TPU v7x, 32 devices: a whole 2x2x4 slice. The times are simulated.
32 devices in a mesh: lon: 4 (over y, x), lat: 8 (over z, core).
Axes of the slice: x: 2, y: 2, z: 4, core: 2. Of those that a mesh axis runs over, the one named last changes fastest.
Arguments:
- tracer: float32 [16, 512, 5760], P(None, 'lat', 'lon'), may hold values from -6 to 6
- zonal_wind: float32 [16, 512, 5760], P(None, 'lat', 'lon'), may hold values from -1 to 1
- meridional_wind: float32 [16, 512, 5760], P(None, 'lat', 'lon'), may hold values from -1 to 1
- cutoff_wave: int32 [512], P('lat'), may hold values from 1 to 127, as said below
- polar_mask: int32 [512], P('lat'), may hold values from 0 to 1, as said below
Outputs:
- advanced: float32 [16, 512, 5760], P(None, 'lat', 'lon')
Inputs may be any that keep to these rules, and one draw needn't show every extreme that they name: `polar_mask`: the rows with value 1 form one contiguous cap at each end of the latitude rows, each cap 512 // 6 rows or somewhat more. `cutoff_wave`: the value is 1 on the first and the last latitude row.
All inputs are finite; a program needn't handle non-finite values.
Results may differ from a plain program's by a relative error of at most 0.0001.
Values sent between devices are 32-bit elements; how exact they have to be, the bound alone decides.
No kernel may reach another device: no remote copies, remote signals or barrier semaphores. Data moves between devices by JAX's collectives and lax.ppermute only.
A program may use at most 192 MiB of HBM per device.

v0:
```python
import math

import jax
import jax.numpy as jnp
from jax import lax
from jax.sharding import PartitionSpec as P

NLON = 5760
KMAX = 128


DIFFUSION = 0.1


def with_halo(cells, sides, width, closed):
    for axis, dim in sides:
        count = lax.axis_size(axis)
        ends = count if closed else count - 1
        head = lax.slice_in_dim(cells, 0, width, axis=dim)
        tail = lax.slice_in_dim(cells, cells.shape[dim] - width, cells.shape[dim], axis=dim)
        cells = jnp.concatenate(
            [
                lax.ppermute(tail, axis, [(i, (i + 1) % count) for i in range(ends)]),
                cells,
                lax.ppermute(head, axis, [((i + 1) % count, i) for i in range(ends)]),
            ],
            axis=dim,
        )
    return cells


def partner_2(block, axis, bit):
    count = lax.axis_size(axis)
    route = []
    for low in range(count):
        high = low | 1 << bit
        if high != low and high < count:
            route += [(low, high), (high, low)]
    return lax.ppermute(block, axis, route)


def wave_table(count, modes, total):
    lon_index = jnp.arange(count, dtype=jnp.int32)
    wave = jnp.arange(modes, dtype=jnp.int32)
    phase = lon_index[:, None] * wave[None, :] % total
    angle = phase.astype(jnp.float32) * (2.0 * math.pi / total)
    return jnp.concatenate([jnp.cos(angle), jnp.sin(angle)], axis=1)


def wave_weights(cutoff_rows, modes, total):
    wave = jnp.arange(modes, dtype=jnp.int32)
    scale = jnp.where(wave == 0, 1.0, 2.0).astype(jnp.float32) / total
    weight = jnp.where(wave[None, :] <= cutoff_rows[:, None], scale[None, :], 0.0)
    return jnp.concatenate([weight, weight], axis=1)


def analyse(row_block, table):
    return jnp.dot(
        row_block, table, precision=lax.Precision.HIGHEST, preferred_element_type=jnp.float32
    )


def synthesise(coefficients, table):
    return jnp.dot(
        coefficients, table.T, precision=lax.Precision.HIGHEST, preferred_element_type=jnp.float32
    )


def tendency_block(state, zonal, meridional):
    flux_x = zonal * state
    flux_y = meridional * state
    lon_pad = with_halo(jnp.stack([state, flux_x]), (("lon", 3),), 1, True)
    both = jnp.stack([state, flux_y])
    lat_pad = with_halo(both, (("lat", 2),), 1, False)
    edges = jnp.concatenate([both[:, :, :1], both[:, :, -1:]], axis=2)
    bit_number = lax.axis_size("lon").bit_length() - 2
    partner = partner_2(edges, "lon", bit_number)
    partner = partner * jnp.array([1.0, -1.0], jnp.float32)[:, None, None, None]
    band = lax.axis_index("lat")
    first_band = band == 0
    last_band = band == lax.axis_size("lat") - 1
    top_row = jnp.where(first_band, partner[:, :, 0:1], lat_pad[:, :, 0:1])
    bottom_row = jnp.where(last_band, partner[:, :, 1:2], lat_pad[:, :, -1:])
    lat_pad = jnp.concatenate([top_row, lat_pad[:, :, 1:-1], bottom_row], axis=2)
    zonal_part = -0.5 * (lon_pad[1, :, :, 2:] - lon_pad[1, :, :, :-2])
    merid_part = -0.5 * (lat_pad[1, :, 2:] - lat_pad[1, :, :-2])
    laplace = (
        lon_pad[0, :, :, 2:]
        + lon_pad[0, :, :, :-2]
        + lat_pad[0, :, 2:]
        + lat_pad[0, :, :-2]
        - 4.0 * state
    )
    return zonal_part + merid_part + DIFFUSION * laplace


def filter_block(moved, cutoff_wave, polar_mask):
    levels, lat_rows, lon_cells = moved.shape
    total_rows = levels * lat_rows
    row_block = moved.reshape(total_rows, lon_cells)
    ways = lax.axis_size("lon")
    circles = lax.all_to_all(row_block, "lon", split_axis=0, concat_axis=1, tiled=True)
    share = total_rows // ways
    row_ids = lax.axis_index("lon") * share + jnp.arange(share, dtype=jnp.int32)
    onehot = (row_ids % lat_rows)[:, None] == jnp.arange(lat_rows, dtype=jnp.int32)[None, :]
    cutoff_rows = jnp.sum(jnp.where(onehot, cutoff_wave[None, :], 0), axis=1)
    table = wave_table(NLON, KMAX, NLON)
    coefficients = analyse(circles, table) * wave_weights(cutoff_rows, KMAX, NLON)
    smooth_circles = synthesise(coefficients, table)
    smooth = lax.all_to_all(smooth_circles, "lon", split_axis=1, concat_axis=0, tiled=True)
    smooth = smooth.reshape(levels, lat_rows, lon_cells)
    return jnp.where(polar_mask[None, :, None] == 1, smooth, moved)


def on_device(tracer, zonal_wind, meridional_wind, cutoff_wave, polar_mask):
    state = tracer
    for substep in range(2):
        moved = state + tendency_block(state, zonal_wind, meridional_wind)
        state = filter_block(moved, cutoff_wave, polar_mask)
    return state


def solution(mesh):
    placed = (
        P(None, "lat", "lon"),
        P(None, "lat", "lon"),
        P(None, "lat", "lon"),
        P("lat"),
        P("lat"),
    )
    return jax.shard_map(
        on_device, mesh=mesh, in_specs=placed, out_specs=P(None, "lat", "lon"), check_vma=False
    )
```

profile of v0, /device:TPU:0, one launch (start us, length us, event | category | flops | bytes accessed | tf_op | source)
XLA Modules:
  0.0 507.5 jit_solution(534814915028234412)
XLA Ops:
  0.0 14.3 %multiply_bitcast_fusion.3 = (f32[1,16,64,1440]{3,2,1,0:T(8,128)}, f32[1,16,64,1440]{3,2,1,0:T(8,128)}) fusion(f32[16,64,1440]{2,1,0:T(8,128)} %param.8, f32[16,64,1440]{2,1,0:T(8,128)} %param.7, f32[16,64,1440]{2,1,0:T(8,128)} %param.9), kind=kLoop, calls=%fused_computation.49 | loop fusion | flops 2949120 | bytes 29491200 | tf_op jit(solution)/shard_map/stack | solution.py:72
  14.3 2.3 fusion.36
  16.6 1.6 collective-permute-start.3
  18.2 3.8 collective-permute-start.4
  22.8 3.9 collective-permute-start
  29.7 2.1 collective-permute-done.1
  33.2 20.0 %pad_maximum_fusion = (f32[2,16,64,1441]{3,2,1,0:T(8,128)}, f32[2,16,64,1441]{3,2,1,0:T(8,128)}) fusion(f32[2,16,64,1]{3,2,1,0:T(8,128)S(1)} %copy.33, f32[1,16,64,1440]{3,2,1,0:T(8,128)} %get-tuple-element.19, f32[1,16,64,1440]{3,2,1,0:T(8,128)} %bitcast.63, f32[2,16,64,1]{3,2,1,0:T(8,128)} %copy.35), kind=kLoop, calls=%fused_computation.5 | loop fusion | flops 11804672 | bytes 35422208 | tf_op jit(solution)/shard_map/concatenate | solution.py:21
  55.8 17.5 %fusion.15 = f32[16,64,1440]{2,1,0:T(8,128)} fusion(f32[16,64,1440]{2,1,0:T(8,128)S(1)} %bitcast.66, f32[2,16,1,1440]{3,2,1,0:T(1,128)S(1)} %get-tuple-element.24, f32[1,16,64,1440]{3,2,1,0:T(8,128)} %get-tuple-element.20, f32[1,16,64,1440]{3,2,1,0:T(8,128)S(1)} %bitcast.67, f32[2,16,1,1440]{3,2,1,0:T(1,128)S(1)} %get-tuple-element.23, ...), kind=kLoop, calls=%fused_computation.35 | loop fusion | flops 29491200 | bytes 47554560 | tf_op jit(solution)/shard_map/add | solution.py:118
  73.3 6.4 %copy.36 = f32[4,256,1440]{1,2,0:T(8,128)} copy(f32[4,256,1440]{2,1,0:T(8,128)} %bitcast.68) | data formatting | bytes 11796480 | tf_op jit(solution)/shard_map/all_to_all | solution.py:102
  79.7 5.5 %all-to-all-start = ((f32[4,256,1440]{1,2,0:T(8,128)}), f32[4,256,1440]{1,2,0:T(8,128)}, u32[]{:S(2)}, u32[]{:S(2)}) async-start(f32[4,256,1440]{1,2,0:T(8,128)} %copy.36), calls=%async_computation | async-start | bytes 11796480 | tf_op jit(solution)/shard_map/all_to_all | solution.py:102
  85.5 13.1 %fusion.24 = (f32[5760,128]{1,0:T(8,128)S(1)}, f32[5760,128]{1,0:T(8,128)}) fusion(), kind=kLoop, calls=%fused_computation.59 | loop fusion | flops 6635520 | bytes 5898240 | tf_op jit(solution)/shard_map/sin | solution.py:47
  98.5 51.9 %all-to-all-done = f32[4,256,1440]{1,2,0:T(8,128)} async-done(((f32[4,256,1440]{1,2,0:T(8,128)}), f32[4,256,1440]{1,2,0:T(8,128)}, u32[]{:S(2)}, u32[]{:S(2)}) %all-to-all-start) | async-done | bytes 5898272 | tf_op jit(solution)/shard_map/all_to_all | solution.py:102
  150.4 13.2 %fusion.31 = f32[256,256]{1,0:T(8,128)S(1)} fusion(f32[256,5760]{0,1:T(8,128)} %bitcast.7, f32[5760,128]{1,0:T(8,128)S(1)} %get-tuple-element.25, f32[5760,128]{1,0:T(8,128)} %get-tuple-element.26, f32[256,128]{1,0:T(8,128)S(1)} %fusion.37), kind=kOutput, calls=%fused_computation.66 | convolution fusion | flops 4531453952 | bytes 12189696 | tf_op jit(solution)/shard_map/dot_general | solution.py:58
  163.6 6.6 %fusion.29 = f32[256,5760]{0,1:T(8,128)} fusion(f32[256,256]{1,0:T(8,128)S(1)} %fusion.31, f32[5760,128]{1,0:T(8,128)S(1)} %get-tuple-element.25, f32[5760,128]{1,0:T(8,128)S(1)} %copy-done.4), kind=kOutput, calls=%fused_computation.64 | convolution fusion | flops 4531322880 | bytes 12058624 | tf_op jit(solution)/shard_map/dot_general | solution.py:64
  170.3 5.7 %all-to-all-start.1 = ((f32[256,4,1440]{0,2,1:T(8,128)}), f32[256,4,1440]{0,2,1:T(8,128)}, u32[]{:S(2)}, u32[]{:S(2)}) async-start(f32[256,4,1440]{0,2,1:T(8,128)} %bitcast.72), calls=%async_computation.1 | async-start | bytes 11796480 | tf_op jit(solution)/shard_map/all_to_all | solution.py:110
  176.0 65.1 %all-to-all-done.1 = f32[256,4,1440]{0,2,1:T(8,128)} async-done(((f32[256,4,1440]{0,2,1:T(8,128)}), f32[256,4,1440]{0,2,1:T(8,128)}, u32[]{:S(2)}, u32[]{:S(2)}) %all-to-all-start.1) | async-done | bytes 5898272 | tf_op jit(solution)/shard_map/all_to_all | solution.py:110
  241.1 6.5 %copy.38 = f32[4,256,1440]{2,1,0:T(8,128)} copy(f32[4,256,1440]{1,2,0:T(8,128)} %bitcast.9) | data formatting | bytes 11796480 | tf_op jit(solution)/shard_map/all_to_all | solution.py:110
  247.6 14.4 %multiply_bitcast_fusion.1 = (f32[1,16,64,1440]{3,2,1,0:T(8,128)}, f32[16,64,1440]{2,1,0:T(8,128)}) fusion(f32[16,64,1440]{2,1,0:T(8,128)} %param.8, f32[16,64,1440]{2,1,0:T(8,128)} %bitcast.70, f32[16,64,1440]{2,1,0:T(8,128)} %fusion.15, pred[64]{0:T(512)(128)(4,1)S(1)} %broadcast_compare_fusion), kind=kLoop, calls=%fused_computation.47 | loop fusion | flops 2949120 | bytes 29491264 | tf_op jit(solution)/shard_map/stack | solution.py:72
  262.0 9.5 %multiply_bitcast_fusion = f32[1,16,64,1440]{3,2,1,0:T(8,128)} fusion(f32[16,64,1440]{2,1,0:T(8,128)} %param.9, f32[16,64,1440]{2,1,0:T(8,128)} %get-tuple-element.6), kind=kLoop, calls=%fused_computation.46 | loop fusion | flops 1474560 | bytes 17694720 | tf_op jit(solution)/shard_map/stack | solution.py:73
  273.1 1.5 collective-permute-start.5
  275.5 2.8 fusion.35
  279.6 2.0 pad_maximum_fusion.22
  281.7 3.7 collective-permute-start.9
  288.6 20.0 %pad_maximum_fusion.1 = (f32[2,16,64,1441]{3,2,1,0:T(8,128)}, f32[2,16,64,1441]{3,2,1,0:T(8,128)}) fusion(f32[2,16,64,1]{3,2,1,0:T(8,128)S(1)} %copy.40, f32[1,16,64,1440]{3,2,1,0:T(8,128)} %get-tuple-element.5, f32[1,16,64,1440]{3,2,1,0:T(8,128)} %bitcast.57, f32[2,16,64,1]{3,2,1,0:T(8,128)} %copy.42), kind=kLoop, calls=%fused_computation.8 | loop fusion | flops 11804672 | bytes 35422208 | tf_op jit(solution)/shard_map/concatenate | solution.py:21
  311.2 17.5 %fusion.5 = f32[16,64,1440]{2,1,0:T(8,128)} fusion(f32[16,64,1440]{2,1,0:T(8,128)S(1)} %bitcast.60, f32[2,16,1,1440]{3,2,1,0:T(1,128)S(1)} %get-tuple-element.22, f32[1,16,64,1440]{3,2,1,0:T(8,128)} %multiply_bitcast_fusion, f32[1,16,64,1440]{3,2,1,0:T(8,128)S(1)} %bitcast.61, f32[2,16,1,1440]{3,2,1,0:T(1,128)S(1)} %get-tuple-element.21, ...), kind=kLoop, calls=%fused_computation.18 | loop fusion | flops 29491200 | bytes 47554560 | tf_op jit(solution)/shard_map/add | solution.py:118
  328.7 6.4 %copy.43 = f32[4,256,1440]{1,2,0:T(8,128)} copy(f32[4,256,1440]{2,1,0:T(8,128)} %bitcast.69) | data formatting | bytes 11796480 | tf_op jit(solution)/shard_map/all_to_all | solution.py:102
  335.1 71.5 %all_to_all.70 = f32[4,256,1440]{1,2,0:T(8,128)S(1)} all-to-all(f32[4,256,1440]{1,2,0:T(8,128)} %copy.43), channel_id=1, replica_groups=mesh['lon'=4,'lat'=8] {'lon'}, dimensions={0} | all-to-all | bytes 11796480 | tf_op jit(solution)/shard_map/all_to_all | solution.py:102
  406.6 10.0 %fusion.32 = f32[256,256]{1,0:T(8,128)S(1)} fusion(f32[256,5760]{0,1:T(8,128)S(1)} %bitcast.74, f32[5760,128]{1,0:T(8,128)S(1)} %copy-done.3, f32[5760,128]{1,0:T(8,128)S(1)} %copy-done.5, f32[256,128]{1,0:T(8,128)S(1)} %fusion.37), kind=kOutput, calls=%fused_computation.67 | convolution fusion | flops 4531453952 | bytes 12189696 | tf_op jit(solution)/shard_map/dot_general | solution.py:58
  416.6 5.0 fusion.27
  421.6 70.2 %all_to_all.71 = f32[256,4,1440]{0,2,1:T(8,128)} all-to-all(f32[256,4,1440]{0,2,1:T(8,128)S(1)} %bitcast.73), channel_id=1, replica_groups=mesh['lon'=4,'lat'=8] {'lon'}, dimensions={1} | all-to-all | bytes 11796480 | tf_op jit(solution)/shard_map/all_to_all | solution.py:110
  491.8 6.5 %copy.45 = f32[4,256,1440]{2,1,0:T(8,128)} copy(f32[4,256,1440]{1,2,0:T(8,128)} %bitcast.75) | data formatting | bytes 11796480 | tf_op jit(solution)/shard_map/all_to_all | solution.py:110
  498.3 9.0 %broadcast_select_fusion = f32[16,64,1440]{2,1,0:T(8,128)} fusion(f32[16,64,1440]{2,1,0:T(8,128)} %bitcast.71, f32[16,64,1440]{2,1,0:T(8,128)} %fusion.5, pred[64]{0:T(512)(128)(4,1)S(1)} %broadcast_compare_fusion), kind=kLoop, calls=%fused_computation.52 | loop fusion | flops 1474560 | bytes 17694784 | tf_op jit(solution)/shard_map/jit(_where)/select_n | solution.py:112
  (66 shorter events, 17.6 us)
Async XLA Ops:
  14.3 7.7 %copy-start.1 = (f32[16,64,1440]{2,1,0:T(8,128)S(1)}, f32[16,64,1440]{2,1,0:T(8,128)}, u32[]{:S(2)}) copy-start(f32[16,64,1440]{2,1,0:T(8,128)} %param.7) | copy-start | bytes 17694724
  14.3 7.7 %copy-start.7 = (f32[1,16,64,1440]{3,2,1,0:T(8,128)S(1)}, f32[1,16,64,1440]{3,2,1,0:T(8,128)}, u32[]{:S(2)}) copy-start(f32[1,16,64,1440]{3,2,1,0:T(8,128)} %get-tuple-element.19) | copy-start | bytes 17694724
  16.6 37.8 %collective-permute-start.3 = (f32[2,16,1,1440]{3,2,1,0:T(1,128)S(1)}, f32[2,16,1,1440]{3,2,1,0:T(1,128)}, u32[]{:S(2)}, u32[]{:S(2)}) collective-permute-start(f32[2,16,1,1440]{3,2,1,0:T(1,128)S(1)} %get-tuple-element.17), channel_id=1, source_target_pairs={{1,0},{2,1},{3,2},{4,3},{5,4},{6,5},{7,6},{9,8},{10,9},{11,10},{12... | collective-permute-start | bytes 552968 | tf_op jit(solution)/shard_map/ppermute | solution.py:25
  18.2 36.3 %collective-permute-start.4 = (f32[2,16,1,1440]{3,2,1,0:T(1,128)S(1)}, f32[2,16,1,1440]{3,2,1,0:T(1,128)}, u32[]{:S(2)}, u32[]{:S(2)}) collective-permute-start(f32[2,16,1,1440]{3,2,1,0:T(1,128)S(1)} %get-tuple-element.18), channel_id=1, source_target_pairs={{0,1},{1,2},{2,3},{3,4},{4,5},{5,6},{6,7},{8,9},{9,10},{10,11},{11... | collective-permute-start | bytes 552968 | tf_op jit(solution)/shard_map/ppermute | solution.py:23
  22.8 6.5 %collective-permute-start = (f32[2,16,64,1]{2,1,3,0:T(8,128)S(1)}, f32[2,16,64,1]{2,1,3,0:T(8,128)S(1)}, u32[]{:S(2)}, u32[]{:S(2)}) collective-permute-start(f32[2,16,64,1]{2,1,3,0:T(8,128)S(1)} %copy.32), channel_id=1, source_target_pairs={{8,0},{16,8},{24,16},{0,24},{9,1},{17,9},{25,17},{1,25},{10,2},{18... | collective-permute-start | bytes 24584 | tf_op jit(solution)/shard_map/ppermute | solution.py:25
  27.1 4.8 collective-permute-start.1
  28.2 25.0 %collective-permute-start.2 = (f32[2,16,2,1440]{3,2,1,0:T(2,128)}, f32[2,16,2,1440]{3,2,1,0:T(2,128)}, u32[]{:S(2)}, u32[]{:S(2)}) collective-permute-start(f32[2,16,2,1440]{3,2,1,0:T(2,128)} %pad_maximum_fusion.21), channel_id=1, source_target_pairs={{0,16},{16,0},{8,24},{24,8},{1,17},{17,1},{9,25},{25,9},{2,18},{18... | collective-permute-start | bytes 1105928 | tf_op jit(solution)/shard_map/ppermute | solution.py:39
  31.8 24.0 %slice-start.2 = ((s8[6291456]{0:T(1024)(128)(4,1)}), s8[2097152]{0:T(1024)(128)(4,1)S(1)}, s32[]{:S(2)}) async-start(s8[6291456]{0:T(1024)(128)(4,1)} %bitcast.65), calls=%async_computation.6 | async-start | bytes 4194304
  33.2 20.0 %copy-start.8 = (f32[2]{0:T(128)S(1)}, f32[2]{0:T(128)}, u32[]{:S(2)}) copy-start(f32[2]{0:T(128)} %constant.67.clone) | copy-start | bytes 28
  33.2 22.6 %slice-start.3 = ((s8[6291456]{0:T(1024)(128)(4,1)}), s8[4194304]{0:T(1024)(128)(4,1)S(1)}, s32[]{:S(2)}) async-start(s8[6291456]{0:T(1024)(128)(4,1)} %bitcast.65), calls=%async_computation.7 | async-start | bytes 8388608
  79.7 5.6 %copy-start.9 = (s32[64]{0:T(128)S(1)}, s32[64]{0:T(128)}, u32[]{:S(2)}) copy-start(s32[64]{0:T(128)} %param.10) | copy-start | bytes 772
  79.7 70.7 %all-to-all-start = ((f32[4,256,1440]{1,2,0:T(8,128)}), f32[4,256,1440]{1,2,0:T(8,128)}, u32[]{:S(2)}, u32[]{:S(2)}) async-start(f32[4,256,1440]{1,2,0:T(8,128)} %copy.36), calls=%async_computation | async-start | bytes 11796480 | tf_op jit(solution)/shard_map/all_to_all | solution.py:102
  98.5 71.7 %copy-start.2 = (f32[5760,128]{1,0:T(8,128)}, f32[5760,128]{1,0:T(8,128)S(1)}, u32[]{:S(2)}) copy-start(f32[5760,128]{1,0:T(8,128)S(1)} %get-tuple-element.25) | copy-start | bytes 8847364
  150.4 13.2 %copy-start.4 = (f32[5760,128]{1,0:T(8,128)S(1)}, f32[5760,128]{1,0:T(8,128)}, u32[]{:S(2)}) copy-start(f32[5760,128]{1,0:T(8,128)} %get-tuple-element.26) | copy-start | bytes 8847364
  170.3 5.7 %copy-start.10 = (s32[64]{0:T(128)S(1)}, s32[64]{0:T(128)}, u32[]{:S(2)}) copy-start(s32[64]{0:T(128)} %param.11) | copy-start | bytes 772
  170.3 70.9 %all-to-all-start.1 = ((f32[256,4,1440]{0,2,1:T(8,128)}), f32[256,4,1440]{0,2,1:T(8,128)}, u32[]{:S(2)}, u32[]{:S(2)}) async-start(f32[256,4,1440]{0,2,1:T(8,128)} %bitcast.72), calls=%async_computation.1 | async-start | bytes 11796480 | tf_op jit(solution)/shard_map/all_to_all | solution.py:110
  262.0 9.5 %copy-start = (f32[16,64,1440]{2,1,0:T(8,128)S(1)}, f32[16,64,1440]{2,1,0:T(8,128)}, u32[]{:S(2)}) copy-start(f32[16,64,1440]{2,1,0:T(8,128)} %get-tuple-element.6) | copy-start | bytes 17694724
  262.0 10.3 %copy-start.6 = (f32[1,16,64,1440]{3,2,1,0:T(8,128)S(1)}, f32[1,16,64,1440]{3,2,1,0:T(8,128)}, u32[]{:S(2)}) copy-start(f32[1,16,64,1440]{3,2,1,0:T(8,128)} %get-tuple-element.5) | copy-start | bytes 17694724
  273.1 13.8 %collective-permute-start.5 = (f32[2,16,64,1]{2,1,3,0:T(8,128)S(1)}, f32[2,16,64,1]{2,1,3,0:T(8,128)S(1)}, u32[]{:S(2)}, u32[]{:S(2)}) collective-permute-start(f32[2,16,64,1]{2,1,3,0:T(8,128)S(1)} %copy.39), channel_id=1, source_target_pairs={{8,0},{16,8},{24,16},{0,24},{9,1},{17,9},{25,17},{1,25},{10,2},{18... | collective-permute-start | bytes 24584 | tf_op jit(solution)/shard_map/ppermute | solution.py:25
  274.9 12.3 %collective-permute-start.6 = (f32[2,16,64,1]{2,1,3,0:T(8,128)S(1)}, f32[2,16,64,1]{2,1,3,0:T(8,128)S(1)}, u32[]{:S(2)}, u32[]{:S(2)}) collective-permute-start(f32[2,16,64,1]{2,1,3,0:T(8,128)S(1)} %copy.41), channel_id=1, source_target_pairs={{0,8},{8,16},{16,24},{24,0},{1,9},{9,17},{17,25},{25,1},{2,10},{10... | collective-permute-start | bytes 24584 | tf_op jit(solution)/shard_map/ppermute | solution.py:23
  278.3 31.5 %collective-permute-start.8 = (f32[2,16,1,1440]{3,2,1,0:T(1,128)}, f32[2,16,1,1440]{3,2,1,0:T(1,128)}, u32[]{:S(2)}, u32[]{:S(2)}) collective-permute-start(f32[2,16,1,1440]{3,2,1,0:T(1,128)} %get-tuple-element.11), channel_id=1, source_target_pairs={{1,0},{2,1},{3,2},{4,3},{5,4},{6,5},{7,6},{9,8},{10,9},{11,10},{12... | collective-permute-start | bytes 552968 | tf_op jit(solution)/shard_map/ppermute | solution.py:25
  281.7 28.2 %collective-permute-start.9 = (f32[2,16,1,1440]{3,2,1,0:T(1,128)S(1)}, f32[2,16,1,1440]{3,2,1,0:T(1,128)}, u32[]{:S(2)}, u32[]{:S(2)}) collective-permute-start(f32[2,16,1,1440]{3,2,1,0:T(1,128)S(1)} %get-tuple-element.12), channel_id=1, source_target_pairs={{0,1},{1,2},{2,3},{3,4},{4,5},{5,6},{6,7},{8,9},{9,10},{10,11},{11... | collective-permute-start | bytes 552968 | tf_op jit(solution)/shard_map/ppermute | solution.py:23
  285.4 23.2 %collective-permute-start.7 = (f32[2,16,2,1440]{3,2,1,0:T(2,128)}, f32[2,16,2,1440]{3,2,1,0:T(2,128)}, u32[]{:S(2)}, u32[]{:S(2)}) collective-permute-start(f32[2,16,2,1440]{3,2,1,0:T(2,128)} %pad_maximum_fusion.22), channel_id=1, source_target_pairs={{0,16},{16,0},{8,24},{24,8},{1,17},{17,1},{9,25},{25,9},{2,18},{18... | collective-permute-start | bytes 1105928 | tf_op jit(solution)/shard_map/ppermute | solution.py:39
  287.3 23.9 %slice-start = ((s8[6291456]{0:T(1024)(128)(4,1)}), s8[2097152]{0:T(1024)(128)(4,1)S(1)}, s32[]{:S(2)}) async-start(s8[6291456]{0:T(1024)(128)(4,1)} %bitcast.59), calls=%async_computation.4 | async-start | bytes 4194304
  288.6 22.6 %slice-start.1 = ((s8[6291456]{0:T(1024)(128)(4,1)}), s8[4194304]{0:T(1024)(128)(4,1)S(1)}, s32[]{:S(2)}) async-start(s8[6291456]{0:T(1024)(128)(4,1)} %bitcast.59), calls=%async_computation.5 | async-start | bytes 8388608
  335.1 71.5 %copy-start.3 = (f32[5760,128]{1,0:T(8,128)S(1)}, f32[5760,128]{1,0:T(8,128)}, u32[]{:S(2)}) copy-start(f32[5760,128]{1,0:T(8,128)} %copy-done.2) | copy-start | bytes 8847364
  335.1 71.5 %copy-start.5 = (f32[5760,128]{1,0:T(8,128)S(1)}, f32[5760,128]{1,0:T(8,128)}, u32[]{:S(2)}) copy-start(f32[5760,128]{1,0:T(8,128)} %get-tuple-element.26) | copy-start | bytes 8847364
where the time goes:
time: 515 us; the launch traced here: 508 us
  other arithmetic  149 us (29%)
  blocking collectives  142 us (28%)
  waiting for transfers between devices  119 us (23%)
  matrix products  34.8 us (7%)
  local copies, waits for them, and re-layouts  31.7 us (6%)
  starting transfers between devices  30.2 us (6%)
    all_to_all x1, blocking collectives, filter_block(): lax.all_to_all(row_block, 'lon', split_axis=0, concat_axis=1, tiled=True)  71.5 us
    all_to_all x1, blocking collectives, filter_block(): lax.all_to_all(smooth_circles, 'lon', split_axis=1, concat_axis=0, tiled=...  70.2 us
    all_to_all x1, waiting for transfers between devices, filter_block(): lax.all_to_all(smooth_circles, 'lon', split_axis=1, concat_axis=0, tiled=...  65.1 us
    all_to_all x1, waiting for transfers between devices, filter_block(): lax.all_to_all(row_block, 'lon', split_axis=0, concat_axis=1, tiled=True)  51.9 us
    concatenate x2, other arithmetic, with_halo(): jnp.concatenate([lax.ppermute(tail, axis, [(i, (i + 1) % count) for i in...  40 us
    add x2, other arithmetic, on_device(): moved = state + tendency_block(state, zonal_wind, meridional_wind)  35 us
    another operation x4, other arithmetic, tendency_block(): lon_pad = with_halo(jnp.stack([state, flux_x]), (('lon', 3),), 1, True)  29.5 us
    dot_general x2, matrix products, analyse(): jnp.dot(row_block, table, precision=lax.Precision.HIGHEST, preferred_elem...  23.2 us
  transfers between devices with their start and end apart: 12, of which 3 were waited for; matrix products, arithmetic and copies ran while one was open for 13% of the time, Pallas kernels for 0%

commit v1 on v0

v1 whole, which is shorter than its diff:
```python
import functools

import jax
import jax.numpy as jnp
import ml_dtypes
import numpy as np
from jax import lax
from jax.experimental import pallas as pl
from jax.experimental.pallas import tpu as pltpu
from jax.sharding import PartitionSpec as P

KMAX = 128
HALF = KMAX // 2
DIFFUSION = 0.1
GROUP = 4
SUB = 8
F32 = jnp.float32
BF16 = jnp.bfloat16
VMEM_LIMIT = 48 * 1024 * 1024


def wide(cells):
    return -(-(cells + 2) // 128) * 128


def split_np(values):
    high = values.astype(ml_dtypes.bfloat16)
    low = (values - high.astype(np.float64)).astype(ml_dtypes.bfloat16)
    return high, low


@functools.lru_cache(maxsize=None)
def wave_tables(cells, ways):
    total = cells * ways
    width = wide(cells)
    lane = np.arange(width)
    start = np.arange(ways)[:, None] * cells
    place = np.where(lane == width - 1, -1, lane)[None, :] + start
    used = (lane <= cells) | (lane == width - 1)
    column = np.arange(2 * KMAX)
    wave = column // KMAX * HALF + column % HALF
    sine = column % KMAX // HALF
    angle = (place[:, :, None] * wave[None, None, :] % total) * (2.0 * np.pi / total)
    table = np.where(sine == 1, np.sin(angle), np.cos(angle))
    project = split_np(np.where(used[None, :, None], table, 0.0))
    inside = np.where((lane < cells)[None, :, None], table, 0.0).transpose(0, 2, 1)
    rebuild = split_np(inside)
    return np.concatenate(project, axis=2), np.concatenate(rebuild, axis=1)


def split(x):
    high = x.astype(BF16)
    return high, (x - high.astype(F32)).astype(BF16)


def project(x, table):
    high, low = split(x)
    both = jnp.dot(high, table, preferred_element_type=F32)
    cross = jnp.dot(low, table[:, : 2 * KMAX], preferred_element_type=F32)
    return both[:, : 2 * KMAX] + both[:, 2 * KMAX :] + cross


def rebuild(coefficients, table):
    high, low = split(coefficients)
    both = jnp.dot(jnp.concatenate([high, high], axis=1), table, preferred_element_type=F32)
    return both + jnp.dot(low, table[: 2 * KMAX], preferred_element_type=F32)


def padded(x, width):
    return jnp.concatenate([x, jnp.zeros((x.shape[0], width - x.shape[1]), F32)], axis=1)


def along_lon(s, u):
    width = s.shape[1]
    spread = DIFFUSION * s
    carry = (0.5 * u) * s
    return (
        (1.0 - 4.0 * DIFFUSION) * s
        + pltpu.roll(spread - carry, width - 1, 1)
        + pltpu.roll(spread + carry, 1, 1)
    )


def moved_rows(s, u, v):
    rows = s.shape[0]
    spread = DIFFUSION * s
    carry = (0.5 * v) * s
    row = lax.broadcasted_iota(jnp.int32, s.shape, 0)
    from_next = jnp.where(row == rows - 1, 0.0, pltpu.roll(spread - carry, rows - 1, 0))
    from_last = jnp.where(row == 0, 0.0, pltpu.roll(spread + carry, 1, 0))
    return along_lon(s, u) + from_next + from_last


def put_halves(ref, at, value):
    for half in range(2):
        ref[half, at, :] = value[:, half * KMAX : (half + 1) * KMAX]


def both_halves(ref, at):
    return jnp.concatenate([ref[0, at, :], ref[1, at, :]], axis=1)


def first_kernel(lon_ref, s_ref, u_ref, v_ref, table_ref, moved_ref, coef_ref):
    del lon_ref
    width = moved_ref.shape[2]
    rows = s_ref.shape[1]
    for g in range(GROUP):
        moved_ref[g] = moved_rows(
            padded(s_ref[g], width), padded(u_ref[g], width), padded(v_ref[g], width)
        )
    x = moved_ref[...].reshape(GROUP * rows, width)
    put_halves(coef_ref, slice(None), project(x, table_ref[...]))


def pack_rows(cut_ref, source_ref, first, out_refs):
    rows = cut_ref.shape[0]

    def body(r, unit):
        cut = cut_ref[r]
        kept = (cut >= 0).astype(jnp.int32)
        more = (cut >= HALF).astype(jnp.int32)

        def put(half, at):
            for part, out_ref in enumerate(out_refs):
                out_ref[at] = source_ref[half, pl.ds(r + part * SUB * rows, SUB, stride=rows), :]

        pl.when(kept == 1)(lambda: put(0, unit))
        pl.when(more == 1)(lambda: put(1, unit + 1))
        return unit + kept + more

    lax.fori_loop(0, rows, body, first)


def weight(half, cut, total):
    lane = lax.broadcasted_iota(jnp.int32, (SUB, KMAX), 1)
    wave = half * HALF + lane % HALF
    scale = jnp.where(wave == 0, 1.0 / total, 2.0 / total)
    return jnp.where(wave <= cut, scale, 0.0)


def unpack_rows(cut_ref, pairs, first, total, out_ref):
    rows = cut_ref.shape[0]
    out_ref[...] = jnp.zeros_like(out_ref)

    def body(r, unit):
        cut = cut_ref[r]
        kept = (cut >= 0).astype(jnp.int32)
        more = (cut >= HALF).astype(jnp.int32)

        def take(half, at):
            scale = weight(half, cut, total)
            for part, (a_ref, b_ref) in enumerate(pairs):
                out_ref[half, pl.ds(r + part * SUB * rows, SUB, stride=rows), :] = (
                    a_ref[at] + b_ref[at]
                ) * scale

        pl.when(kept == 1)(lambda: take(0, unit))
        pl.when(more == 1)(lambda: take(1, unit + 1))
        return unit + kept + more

    lax.fori_loop(0, rows, body, first)


def join_kernel(
    lon_ref, cut_ref, coef_ref, mine_ref, north_ref, south_ref, table_ref,
    flow_ref, a_ref, b_ref, sum_ref,
):
    del lon_ref
    rows = cut_ref.shape[0]
    levels = coef_ref.shape[1] // rows

    def down(s, v):
        return DIFFUSION * s + (0.5 * v) * s

    def up(s, v):
        return DIFFUSION * s - (0.5 * v) * s

    flow_ref[0] = down(north_ref[0], north_ref[2])
    flow_ref[1] = up(south_ref[0], south_ref[2])
    flow_ref[2] = along_lon(north_ref[0], north_ref[1]) + north_ref[3] + up(mine_ref[0], mine_ref[1])
    flow_ref[3] = along_lon(south_ref[0], south_ref[1]) + south_ref[3] + down(mine_ref[2], mine_ref[3])
    extra = project(flow_ref[...].reshape(4 * levels, flow_ref.shape[2]), table_ref[...])
    sum_ref[...] = coef_ref[...]
    for part, out_ref in enumerate((a_ref, b_ref)):
        at = part * SUB
        first = pl.ds(at * rows, SUB, stride=rows)
        last = pl.ds(at * rows + rows - 1, SUB, stride=rows)
        for half in range(2):
            cols = slice(half * KMAX, (half + 1) * KMAX)
            sum_ref[half, first, :] = sum_ref[half, first, :] + extra[at : at + SUB, cols]
            sum_ref[half, last, :] = sum_ref[half, last, :] + extra[levels + at : levels + at + SUB, cols]
            out_ref[half] = extra[2 * levels + at : 2 * levels + at + SUB, cols]
            out_ref[2 + half] = extra[3 * levels + at : 3 * levels + at + SUB, cols]
    pack_rows(cut_ref, sum_ref, 4, (a_ref, b_ref))


def second_kernel(
    total, cells,
    lon_ref, cut_ref, a0_ref, a1_ref, b0_ref, b1_ref, flow_ref, edge_cut_ref, edge_fix_ref, edge_v_ref,
    moved_ref, fix_ref, mask_ref, u_ref, v_ref, table_ref, back_ref,
    out_ref, a_ref, b_ref, coef_ref, sum_ref, step_ref, edge_ref,
):
    del lon_ref
    step = pl.program_id(0)
    rows = cut_ref.shape[0]
    width = out_ref.shape[2]
    levels = step_ref.shape[1]
    pairs = ((a0_ref, a1_ref), (b0_ref, b1_ref))

    @pl.when(step == 0)
    def _():
        unpack_rows(cut_ref, pairs, 4, total, coef_ref)
        for side in range(2):
            for part, (x_ref, y_ref) in enumerate(pairs):
                at = side * levels + part * SUB
                for half in range(2):
                    scale = weight(half, edge_cut_ref[side, :, :], total)
                    edge_ref[at : at + SUB, half * KMAX : (half + 1) * KMAX] = (
                        x_ref[2 * side + half] + y_ref[2 * side + half]
                    ) * scale
        smooth = rebuild(edge_ref[...], back_ref[...])
        lane = lax.broadcasted_iota(jnp.int32, (levels, width), 1)
        for side in range(2):
            plain = flow_ref[2 + side]
            plain = jnp.where(lane == 0, plain + edge_fix_ref[side, :, 0:1], plain)
            plain = jnp.where(lane == cells - 1, plain + edge_fix_ref[side, :, 1:2], plain)
            plain = jnp.where(lane < cells, plain, 0.0)
            filtered = edge_cut_ref[side, 0:1, 0:1] >= 0
            s = jnp.where(filtered, smooth[side * levels : (side + 1) * levels], plain)
            carry = (0.5 * edge_v_ref[side]) * s
            step_ref[side] = DIFFUSION * s + (carry if side == 0 else -carry)

    smooth = rebuild(both_halves(coef_ref, pl.ds(step * (GROUP * rows), GROUP * rows)), back_ref[...])
    lane = lax.broadcasted_iota(jnp.int32, (rows, width), 1)
    row = lax.broadcasted_iota(jnp.int32, (rows, width), 0)
    filtered = mask_ref[...] == 1
    for g in range(GROUP):
        level = step * GROUP + g
        plain = moved_ref[g]
        plain = plain + jnp.where(row == 0, flow_ref[0, pl.ds(level, 1), :], 0.0)
        plain = plain + jnp.where(row == rows - 1, flow_ref[1, pl.ds(level, 1), :], 0.0)
        plain = plain + jnp.where(lane == 0, fix_ref[g][:, 0:1], 0.0)
        plain = plain + jnp.where(lane == cells - 1, fix_ref[g][:, 1:2], 0.0)
        plain = jnp.where(lane < cells, plain, 0.0)
        s = jnp.where(filtered, smooth[g * rows : (g + 1) * rows], plain)
        moved = moved_rows(s, padded(u_ref[g], width), padded(v_ref[g], width))
        moved = moved + jnp.where(row == 0, step_ref[0, pl.ds(level, 1), :], 0.0)
        moved = moved + jnp.where(row == rows - 1, step_ref[1, pl.ds(level, 1), :], 0.0)
        out_ref[g] = moved
    x = out_ref[...].reshape(GROUP * rows, width)
    put_halves(sum_ref, pl.ds(step * (GROUP * rows), GROUP * rows), project(x, table_ref[...]))

    @pl.when(step == pl.num_programs(0) - 1)
    def _():
        pack_rows(cut_ref, sum_ref, 0, (a_ref, b_ref))


def third_kernel(
    total, cells,
    lon_ref, cut_ref, a0_ref, a1_ref, b0_ref, b1_ref, moved_ref, fix_ref, mask_ref, back_ref,
    out_ref, coef_ref,
):
    del lon_ref
    step = pl.program_id(0)
    rows = cut_ref.shape[0]
    width = moved_ref.shape[2]

    @pl.when(step == 0)
    def _():
        unpack_rows(cut_ref, ((a0_ref, a1_ref), (b0_ref, b1_ref)), 0, total, coef_ref)

    smooth = rebuild(both_halves(coef_ref, pl.ds(step * (GROUP * rows), GROUP * rows)), back_ref[...])
    lane = lax.broadcasted_iota(jnp.int32, (rows, width), 1)
    filtered = mask_ref[...] == 1
    for g in range(GROUP):
        plain = moved_ref[g]
        plain = plain + jnp.where(lane == 0, fix_ref[g][:, 0:1], 0.0)
        plain = plain + jnp.where(lane == cells - 1, fix_ref[g][:, 1:2], 0.0)
        out_ref[g] = jnp.where(filtered, smooth[g * rows : (g + 1) * rows], plain)[:, :cells]


def whole(shape):
    return pl.BlockSpec(shape, lambda *_: (0,) * len(shape))


def by_group(shape):
    return pl.BlockSpec((GROUP, *shape[1:]), lambda i, *_: (i, 0, 0))


def own_table(shape):
    return pl.BlockSpec((None, *shape[1:]), lambda i, lon, *_: (lon[0], 0, 0))


def call(kernel, steps, prefetch, inputs, outputs, scratch):
    return pl.pallas_call(
        kernel,
        grid_spec=pltpu.PrefetchScalarGridSpec(
            num_scalar_prefetch=len(prefetch),
            grid=(steps,),
            in_specs=[spec for _, spec in inputs],
            out_specs=[spec for _, spec in outputs],
            scratch_shapes=scratch,
        ),
        out_shape=[jax.ShapeDtypeStruct(shape, F32) for shape, _ in outputs],
        compiler_params=pltpu.CompilerParams(vmem_limit_bytes=VMEM_LIMIT),
    )(*prefetch, *[array for array, _ in inputs])


def swap(x, bit):
    count = lax.axis_size("lon")
    return lax.ppermute(x, "lon", [(i, i ^ (1 << bit)) for i in range(count)])


def sum_over_lon(a, b):
    bits = lax.axis_size("lon").bit_length() - 1
    for i in range(bits):
        a_in, b_in = swap(a, i), swap(b, bits - 1 - i)
        if i == bits - 1:
            return a, a_in, b, b_in
        a, b = a + a_in, b + b_in


def lat_ring(bands, ways, turn):
    pairs = []
    for band in range(bands):
        for l in range(ways):
            east = l < ways // 2
            other = (l + ways // 2) % ways
            step = 1 if east == (turn == 0) else -1
            to = (band + step, l) if 0 <= band + step < bands else (band, other)
            pairs.append((l * bands + band, to[1] * bands + to[0]))
    return pairs


def lon_edges(moved, cells):
    ways = lax.axis_size("lon")
    west = lax.ppermute(moved[..., cells], "lon", [(i, (i + 1) % ways) for i in range(ways)])
    east = lax.ppermute(moved[..., -1], "lon", [(i, (i - 1) % ways) for i in range(ways)])
    return jnp.stack([west, east], axis=-1)


def on_device(tracer, zonal, meridional, cutoff_wave, polar_mask):
    levels, rows, cells = tracer.shape
    ways, bands = lax.axis_size("lon"), lax.axis_size("lat")
    width = wide(cells)
    total = cells * ways
    tables = wave_tables(cells, ways)
    table, back = jnp.asarray(tables[0]), jnp.asarray(tables[1])
    lon = lax.axis_index("lon").reshape(1)
    band = lax.axis_index("lat")
    cut = jnp.where(polar_mask == 1, cutoff_wave, -1)
    mask = polar_mask[:, None]
    steps = levels // GROUP

    def edge_rows(at, beyond, sign):
        s, v = tracer[:, beyond], meridional[:, beyond]
        out = jnp.stack(
            [tracer[:, at], zonal[:, at], meridional[:, at], DIFFUSION * s + sign * (0.5 * v) * s]
        )
        tail = jnp.full((4, levels, width - cells), cut[at].astype(F32))
        return jnp.concatenate([out, tail], axis=2)

    top, bottom = edge_rows(0, 1, -1.0), edge_rows(rows - 1, rows - 2, 1.0)
    near = lon[0] < ways // 2
    ring = ("lon", "lat")
    got0 = lax.ppermute(jnp.where(near, bottom, top), ring, lat_ring(bands, ways, 0))
    got1 = lax.ppermute(jnp.where(near, top, bottom), ring, lat_ring(bands, ways, 1))

    moved, coef = call(
        first_kernel, steps, (lon,),
        [(tracer, by_group(tracer.shape)), (zonal, by_group(tracer.shape)), (meridional, by_group(tracer.shape)),
         (table, own_table(table.shape))],
        [((levels, rows, width), by_group((levels, rows, width))),
         ((2, levels * rows, KMAX), pl.BlockSpec((2, GROUP * rows, KMAX), lambda i, *_: (0, i, 0)))],
        [],
    )

    north = jnp.where(near, got0, got1)
    south = jnp.where(near, got1, got0)
    edge_cut = jnp.stack([north[0, 0, cells], south[0, 0, cells]]).astype(jnp.int32)
    edge_cut = jnp.broadcast_to(edge_cut[:, None, None], (2, SUB, KMAX))
    inside = jnp.arange(width) < cells
    turn = jnp.array([1.0, 1.0, -1.0, 1.0], F32)[:, None, None]
    north = jnp.where(inside, jnp.where(band == 0, turn, 1.0) * north, 0.0)
    south = jnp.where(inside, jnp.where(band == bands - 1, turn, 1.0) * south, 0.0)
    mine = jnp.where(inside, jnp.stack([top[0], top[2], bottom[0], bottom[2]]), 0.0)
    edge_v = jnp.stack([north[2], south[2]])

    units = 2 * rows + 4
    flow, a, b = call(
        join_kernel, 1, (lon, cut),
        [(coef, whole(coef.shape)), (mine, whole(mine.shape)),
         (north, whole(north.shape)), (south, whole(south.shape)), (table, own_table(table.shape))],
        [((4, levels, width), whole((4, levels, width))), ((units, SUB, KMAX), whole((units, SUB, KMAX))),
         ((units, SUB, KMAX), whole((units, SUB, KMAX)))],
        [pltpu.VMEM((2, levels * rows, KMAX), F32)],
    )
    sums = sum_over_lon(a, b)
    fix = lon_edges(jnp.concatenate([moved, flow[2:].transpose(1, 0, 2)], axis=1)[:, :, cells - 1 :], 1)
    edge_fix = fix[:, rows:].transpose(1, 0, 2)
    fix = fix[:, :rows]

    moved, a, b = call(
        functools.partial(second_kernel, total, cells), steps, (lon, cut),
        [*[(x, whole(x.shape)) for x in (*sums, flow, edge_cut, edge_fix, edge_v)],
         (moved, by_group(moved.shape)), (fix, by_group(fix.shape)), (mask, whole(mask.shape)),
         (zonal, by_group(tracer.shape)), (meridional, by_group(tracer.shape)),
         (table, own_table(table.shape)), (back, own_table(back.shape))],
        [((levels, rows, width), by_group((levels, rows, width))), ((2 * rows, SUB, KMAX), whole((2 * rows, SUB, KMAX))),
         ((2 * rows, SUB, KMAX), whole((2 * rows, SUB, KMAX)))],
        [pltpu.VMEM((2, levels * rows, KMAX), F32), pltpu.VMEM((2, levels * rows, KMAX), F32),
         pltpu.VMEM((2, levels, width), F32), pltpu.VMEM((2 * levels, 2 * KMAX), F32)],
    )
    sums = sum_over_lon(a, b)
    fix = lon_edges(moved, cells)

    (out,) = call(
        functools.partial(third_kernel, total, cells), steps, (lon, cut),
        [*[(x, whole(x.shape)) for x in sums], (moved, by_group(moved.shape)), (fix, by_group(fix.shape)),
         (mask, whole(mask.shape)), (back, own_table(back.shape))],
        [(tracer.shape, by_group(tracer.shape))],
        [pltpu.VMEM((2, levels * rows, KMAX), F32)],
    )
    return out


def solution(mesh):
    placed = (
        P(None, "lat", "lon"),
        P(None, "lat", "lon"),
        P(None, "lat", "lon"),
        P("lat"),
        P("lat"),
    )
    return jax.shard_map(
        on_device, mesh=mesh, in_specs=placed, out_specs=P(None, "lat", "lon"), check_vma=False
    )
```

time: 515 us -> 125 us (0.24); the launches traced: 508 us -> 125 us
  other arithmetic: 149 us -> 2.78 us
  blocking collectives: 142 us -> 0 us
  waiting for transfers between devices: 119 us -> 38 us
  Pallas kernels: 0 us -> 50.1 us
  matrix products: 34.8 us -> 0 us
  local copies, waits for them, and re-layouts: 31.7 us -> 15.4 us
  starting transfers between devices: 30.2 us -> 17.5 us
    all_to_all x2 -> x0, blocking collectives: 142 us -> none  [the longest x1 71.5 us: filter_block(): lax.all_to_all(row_block, 'lon', split_axis=0, concat_axis=1, tiled=True)]
    all_to_all x2 -> x0, waiting for transfers between devices: 117 us -> none  [the longest x1 65.1 us: filter_block(): lax.all_to_all(smooth_circles, 'lon', split_axis=1, concat_axis=0, tiled=...]
    pallas_call x0 -> x4, Pallas kernels: none -> 50.1 us  [call(): pl.pallas_call(kernel, grid_spec=pltpu.PrefetchScalarGridSpec(num_scalar_...]
    another operation x7 -> x4, other arithmetic: 44 us -> 0.1 us  [the longest x3 0.08 us: lon_edges(): return jnp.stack([west, east], axis=-1)]
    concatenate x4 -> x0, other arithmetic: 43.1 us -> none  [the longest x2 40 us: with_halo(): jnp.concatenate([lax.ppermute(tail, axis, [(i, (i + 1) % count) for i in...]
    ppermute x10 -> x14, waiting for transfers between devices: 2.15 us -> 38 us  [the longest x8 31.1 us: swap(): return lax.ppermute(x, 'lon', [(i, i ^ 1 << bit) for i in range(count)])]
    dot_general x4 -> x0, matrix products: 34.8 us -> none  [the longest x2 23.2 us: analyse(): jnp.dot(row_block, table, precision=lax.Precision.HIGHEST, preferred_elem...]
    add x2 -> x6, other arithmetic: 35 us -> 0.28 us  [the longest x4 0.22 us: sum_over_lon(): a, b = (a + a_in, b + b_in)]
  transfers between devices with their start and end apart: 12 -> 14, of which waited for: 3 -> 6; matrix products, arithmetic and copies ran while one was open for 13% -> 7% of each run, Pallas kernels for 0% -> 10%
where the time goes in v1:
time: 125 us
  Pallas kernels  50.1 us (40%)
  waiting for transfers between devices  38 us (30%)
  starting transfers between devices  17.5 us (14%)
  local copies, waits for them, and re-layouts  15.4 us (12%)
  other arithmetic  2.78 us (2%)
  between operations  1.5 us (1%)
    pallas_call x4, Pallas kernels, call(): pl.pallas_call(kernel, grid_spec=pltpu.PrefetchScalarGridSpec(num_scalar_...  50.1 us
    ppermute x8, waiting for transfers between devices, swap(): return lax.ppermute(x, 'lon', [(i, i ^ 1 << bit) for i in range(count)])  31.1 us
    ppermute x8, starting transfers between devices, swap(): return lax.ppermute(x, 'lon', [(i, i ^ 1 << bit) for i in range(count)])  8.44 us
    ppermute x2, waiting for transfers between devices, lon_edges(): lax.ppermute(moved[..., cells], 'lon', [(i, (i + 1) % ways) for i in rang...  6.91 us
    ppermute x2, starting transfers between devices, lon_edges(): lax.ppermute(moved[..., -1], 'lon', [(i, (i - 1) % ways) for i in range(w...  3.93 us
    unnamed x7, local copies, waits for them, and re-layouts  3.9 us
    slice x2, local copies, waits for them, and re-layouts, lon_edges(): moved[..., cells]  2.8 us
    ppermute x1, starting transfers between devices, on_device(): lax.ppermute(jnp.where(near, top, bottom), ring, lat_ring(bands, ways, 1))  2.59 us
  transfers between devices with their start and end apart: 14, of which 6 were waited for; matrix products, arithmetic and copies ran while one was open for 7% of the time, Pallas kernels for 10%

profile of v1, /device:TPU:0, one launch (start us, length us, event | category | flops | bytes accessed | tf_op | source)
XLA Modules:
  0.0 125.3 jit_solution(14337972971213314925)
XLA Ops:
  0.0 0.7 compare_select_fusion.cut_ref
  0.7 0.6 fusion.9
  2.6 1.5 %fusion.5 = (f32[16,1,1440]{2,1,0:T(1,128)S(1)}, f32[16,1,1440]{2,1,0:T(1,128)S(1)}) fusion(f32[16,64,1440]{2,1,0:T(8,128)} %u_ref.3), kind=kLoop, calls=%fused_computation.45 | loop fusion | bytes 368640 | tf_op jit(solution)/shard_map/slice | solution.py:358
  4.1 2.3 %fusion.4 = (f32[16,1,1440]{2,1,0:T(1,128)S(1)}, f32[16,1,1440]{2,1,0:T(1,128)S(1)}, f32[16,1,1440]{2,1,0:T(1,128)S(1)}, f32[16,1,1440]{2,1,0:T(1,128)S(1)}) fusion(f32[16,64,1440]{2,1,0:T(8,128)} %s_ref.1), kind=kLoop, calls=%fused_computation.44 | loop fusion | bytes 737280 | tf_op jit(solution)/shard_map/slice | solution.py:358
  6.4 2.3 %fusion.6 = (f32[16,1,1440]{2,1,0:T(1,128)S(1)}, f32[16,1,1440]{2,1,0:T(1,128)S(1)}, f32[16,1,1440]{2,1,0:T(1,128)S(1)}, f32[16,1,1440]{2,1,0:T(1,128)S(1)}) fusion(f32[16,64,1440]{2,1,0:T(8,128)} %v_ref.3), kind=kLoop, calls=%fused_computation.46 | loop fusion | bytes 737280 | tf_op jit(solution)/shard_map/slice | solution.py:358
  9.5 2.6 %collective-permute-start.1 = (f32[4,16,1536]{2,1,0:T(8,128)S(1)}, f32[4,16,1536]{2,1,0:T(8,128)S(1)}, u32[]{:S(2)}, u32[]{:S(2)}) collective-permute-start(f32[4,16,1536]{2,1,0:T(8,128)S(1)} %get-tuple-element.29), channel_id=1, source_target_pairs={{0,16},{8,24},{16,17},{24,25},{1,0},{9,8},{17,18},{25,26},{2,1},{1... | collective-permute-start | bytes 1179656 | tf_op jit(solution)/shard_map/ppermute | solution.py:367
  12.3 12.4 %shard_map.82 = (f32[16,64,1536]{2,1,0:T(8,128)}, f32[2,1024,128]{2,1,0:T(8,128)S(1)}) custom-call(s32[1]{0:T(128)} %bitcast.lon_ref, f32[16,64,1440]{2,1,0:T(8,128)} %s_ref.1, f32[16,64,1440]{2,1,0:T(8,128)} %u_ref.3, f32[16,64,1440]{2,1,0:T(8,128)} %v_ref.3, bf16[4,1536,512]{2,1,0:T(8,128)(2,1)} %constant.37.clone.table_ref), custom_call_target="tpu_custom_call" | custom-call | tf_op jit(solution)/shard_map/pallas_call | solution.py:295
  24.7 3.4 %constant_dynamic-update-slice_fusion = f32[16,66,1536]{2,1,0:T(8,128)S(1)} fusion(f32[16,64,1536]{2,1,0:T(8,128)} %get-tuple-element.17.moved_ref), kind=kLoop, calls=%fused_computation.39 | loop fusion | bytes 12582912
  28.3 0.6 slice.115
  29.0 0.6 slice.116
  29.6 4.5 %shard_map.83 = (f32[4,16,1536]{2,1,0:T(8,128)S(1)}, f32[132,8,128]{2,1,0:T(8,128)S(1)}, f32[132,8,128]{2,1,0:T(8,128)S(1)}) custom-call(s32[1]{0:T(128)} %bitcast.lon_ref, s32[64]{0:T(128)S(1)} %compare_select_fusion.cut_ref, f32[2,1024,128]{2,1,0:T(8,128)S(1)} %get-tuple-element.13.coef_ref, f32[4,16,1536]{2,1,0:T(8,128)S(1)} %get-tuple-element.48.mine_ref, ...), custom_call_target="tpu_custom_call" | custom-call | tf_op jit(solution)/shard_map/pallas_call | solution.py:295
  34.1 2.0 %collective-permute-start.2 = (f32[132,8,128]{2,1,0:T(8,128)S(1)}, f32[132,8,128]{2,1,0:T(8,128)S(1)}, u32[]{:S(2)}, u32[]{:S(2)}) collective-permute-start(f32[132,8,128]{2,1,0:T(8,128)S(1)} %get-tuple-element.14), channel_id=1, source_target_pairs={{0,8},{8,0},{16,24},{24,16},{1,9},{9,1},{17,25},{25,17},{2,10},{10... | collective-permute-start | bytes 1622024 | tf_op jit(solution)/shard_map/ppermute | solution.py:311
  36.3 0.9 slice_reduce_fusion.1
  37.3 0.6 collective-permute-start.6
  37.9 2.4 %collective-permute-start.7 = (f32[16,66]{1,0:T(8,128)S(1)}, f32[16,66]{1,0:T(8,128)S(1)}, u32[]{:S(2)}, u32[]{:S(2)}) collective-permute-start(f32[16,66]{1,0:T(8,128)S(1)} %get-tuple-element.22), channel_id=1, source_target_pairs={{0,24},{8,0},{16,8},{24,16},{1,25},{9,1},{17,9},{25,17},{2,26},{10... | collective-permute-start | bytes 12680 | tf_op jit(solution)/shard_map/ppermute | solution.py:338
  40.3 8.4 %collective-permute-done.2 = f32[132,8,128]{2,1,0:T(8,128)S(1)} collective-permute-done((f32[132,8,128]{2,1,0:T(8,128)S(1)}, f32[132,8,128]{2,1,0:T(8,128)S(1)}, u32[]{:S(2)}, u32[]{:S(2)}) %collective-permute-start.2) | collective-permute-done | bytes 540704 | tf_op jit(solution)/shard_map/ppermute | solution.py:311
  48.7 0.8 collective-permute-start.3
  50.0 1.2 collective-permute-start.5
  51.2 1.3 %maximum_convert_fusion = s32[2]{0:T(128)S(1)} fusion(f32[1]{0:T(128)} %bitcast.12, f32[1]{0:T(128)} %bitcast.11), kind=kLoop, calls=%fused_computation.43 | loop fusion | flops 4 | bytes 16 | tf_op jit(solution)/shard_map/convert_element_type | solution.py:380
  53.1 9.6 %collective-permute-done.3.a1_ref = f32[132,8,128]{2,1,0:T(8,128)S(1)} collective-permute-done((f32[132,8,128]{2,1,0:T(8,128)S(1)}, f32[132,8,128]{2,1,0:T(8,128)S(1)}, u32[]{:S(2)}, u32[]{:S(2)}) %collective-permute-start.3) | collective-permute-done | bytes 540704 | tf_op jit(solution)/shard_map/ppermute | solution.py:311
  62.6 1.6 %collective-permute-done.5.b1_ref = f32[132,8,128]{2,1,0:T(8,128)S(1)} collective-permute-done((f32[132,8,128]{2,1,0:T(8,128)S(1)}, f32[132,8,128]{2,1,0:T(8,128)S(1)}, u32[]{:S(2)}, u32[]{:S(2)}) %collective-permute-start.5) | collective-permute-done | bytes 540704 | tf_op jit(solution)/shard_map/ppermute | solution.py:311
  64.3 23.0 %shard_map.84 = (f32[16,64,1536]{2,1,0:T(8,128)}, f32[128,8,128]{2,1,0:T(8,128)S(1)}, f32[128,8,128]{2,1,0:T(8,128)S(1)}) custom-call(s32[1]{0:T(128)} %bitcast.lon_ref, s32[64]{0:T(128)S(1)} %compare_select_fusion.cut_ref, f32[132,8,128]{2,1,0:T(8,128)S(1)} %add.46.a0_ref, f32[132,8,128]{2,1,0:T(8,128)S(1)} %collective-permute-done.3.a1_ref, ...), custom_call_target="tpu_custom_call" | custom-call | tf_op jit(solution)/shard_map/pallas_call | solution.py:295
  87.3 1.5 %collective-permute-start.8 = (f32[128,8,128]{2,1,0:T(8,128)S(1)}, f32[128,8,128]{2,1,0:T(8,128)S(1)}, u32[]{:S(2)}, u32[]{:S(2)}) collective-permute-start(f32[128,8,128]{2,1,0:T(8,128)S(1)} %get-tuple-element.18), channel_id=1, source_target_pairs={{0,8},{8,0},{16,24},{24,16},{1,9},{9,1},{17,25},{25,17},{2,10},{10... | collective-permute-start | bytes 1572872 | tf_op jit(solution)/shard_map/ppermute | solution.py:311
  88.8 0.6 collective-permute-start.10
  89.3 11.1 %collective-permute-done.8 = f32[128,8,128]{2,1,0:T(8,128)S(1)} collective-permute-done((f32[128,8,128]{2,1,0:T(8,128)S(1)}, f32[128,8,128]{2,1,0:T(8,128)S(1)}, u32[]{:S(2)}, u32[]{:S(2)}) %collective-permute-start.8) | collective-permute-done | bytes 524320 | tf_op jit(solution)/shard_map/ppermute | solution.py:311
  100.5 1.7 %collective-permute-start.9 = (f32[128,8,128]{2,1,0:T(8,128)S(1)}, f32[128,8,128]{2,1,0:T(8,128)S(1)}, u32[]{:S(2)}, u32[]{:S(2)}) collective-permute-start(f32[128,8,128]{2,1,0:T(8,128)S(1)} %add.48.a0_ref), channel_id=1, source_target_pairs={{0,16},{8,24},{16,0},{24,8},{1,17},{9,25},{17,1},{25,9},{2,18},{10... | collective-permute-start | bytes 1572872 | tf_op jit(solution)/shard_map/ppermute | solution.py:311
  102.2 0.7 collective-permute-start.11
  102.9 1.9 %slice_reduce_fusion.3 = (f32[16,64]{1,0:T(8,128)S(1)}, f32[16,64]{1,0:T(8,128)S(1)}) fusion(f32[16,64,1536]{2,1,0:T(8,128)} %get-tuple-element.20.moved_ref), kind=kLoop, calls=%fused_computation.3 | loop fusion | bytes 16384 | tf_op jit(solution)/shard_map/slice | solution.py:337
  104.8 1.4 %collective-permute-start.12 = (f32[16,64]{1,0:T(8,128)S(1)}, f32[16,64]{1,0:T(8,128)S(1)}, u32[]{:S(2)}, u32[]{:S(2)}) collective-permute-start(f32[16,64]{1,0:T(8,128)S(1)} %get-tuple-element.23), channel_id=1, source_target_pairs={{0,8},{8,16},{16,24},{24,0},{1,9},{9,17},{17,25},{25,1},{2,10},{10... | collective-permute-start | bytes 12296 | tf_op jit(solution)/shard_map/ppermute | solution.py:337
  106.3 1.5 %collective-permute-start.13 = (f32[16,64]{1,0:T(8,128)S(1)}, f32[16,64]{1,0:T(8,128)S(1)}, u32[]{:S(2)}, u32[]{:S(2)}) collective-permute-start(f32[16,64]{1,0:T(8,128)S(1)} %get-tuple-element.24), channel_id=1, source_target_pairs={{0,24},{8,0},{16,8},{24,16},{1,25},{9,1},{17,9},{25,17},{2,26},{10... | collective-permute-start | bytes 12296 | tf_op jit(solution)/shard_map/ppermute | solution.py:338
  107.8 6.9 %collective-permute-done.12 = f32[16,64]{1,0:T(8,128)S(1)} collective-permute-done((f32[16,64]{1,0:T(8,128)S(1)}, f32[16,64]{1,0:T(8,128)S(1)}, u32[]{:S(2)}, u32[]{:S(2)}) %collective-permute-start.12) | collective-permute-done | bytes 4128 | tf_op jit(solution)/shard_map/ppermute | solution.py:337
  115.0 10.3 %shard_map.85 = f32[16,64,1440]{2,1,0:T(8,128)} custom-call(s32[1]{0:T(128)} %bitcast.lon_ref, s32[64]{0:T(128)S(1)} %compare_select_fusion.cut_ref, f32[128,8,128]{2,1,0:T(8,128)S(1)} %add.48.a0_ref, f32[128,8,128]{2,1,0:T(8,128)S(1)} %collective-permute-done.9.a1_ref, f32[128,8,128]{2,1,0:T(8,128)S(1)} %add.49.b0_ref, ...), custom_call_target="tpu_custom_call" | custom-call | tf_op jit(solution)/shard_map/pallas_call | solution.py:295
  (43 shorter events, 2.8 us)
Async XLA Ops:
  0.0 12.2 %copy-start = (s32[64]{0:T(128)S(1)}, s32[64]{0:T(128)}, u32[]{:S(2)}) copy-start(s32[64]{0:T(128)} %param.12) | copy-start | bytes 772
  9.0 19.1 %collective-permute-start = (f32[4,16,1536]{2,1,0:T(8,128)S(1)}, f32[4,16,1536]{2,1,0:T(8,128)S(1)}, u32[]{:S(2)}, u32[]{:S(2)}) collective-permute-start(f32[4,16,1536]{2,1,0:T(8,128)S(1)} %broadcast_select_fusion.3), channel_id=1, source_target_pairs={{0,1},{8,9},{16,0},{24,8},{1,2},{9,10},{17,16},{25,24},{2,3},{10,1... | collective-permute-start | bytes 1179656 | tf_op jit(solution)/shard_map/ppermute | solution.py:366
  9.5 18.6 %collective-permute-start.1 = (f32[4,16,1536]{2,1,0:T(8,128)S(1)}, f32[4,16,1536]{2,1,0:T(8,128)S(1)}, u32[]{:S(2)}, u32[]{:S(2)}) collective-permute-start(f32[4,16,1536]{2,1,0:T(8,128)S(1)} %get-tuple-element.29), channel_id=1, source_target_pairs={{0,16},{8,24},{16,17},{24,25},{1,0},{9,8},{17,18},{25,26},{2,1},{1... | collective-permute-start | bytes 1179656 | tf_op jit(solution)/shard_map/ppermute | solution.py:367
  12.3 12.4 %copy-start.1 = (f32[4]{0:T(128)S(1)}, f32[4]{0:T(128)}, u32[]{:S(2)}) copy-start(f32[4]{0:T(128)} %constant.39.clone) | copy-start | bytes 52
  34.1 14.6 %collective-permute-start.2 = (f32[132,8,128]{2,1,0:T(8,128)S(1)}, f32[132,8,128]{2,1,0:T(8,128)S(1)}, u32[]{:S(2)}, u32[]{:S(2)}) collective-permute-start(f32[132,8,128]{2,1,0:T(8,128)S(1)} %get-tuple-element.14), channel_id=1, source_target_pairs={{0,8},{8,0},{16,24},{24,16},{1,9},{9,1},{17,25},{25,17},{2,10},{10... | collective-permute-start | bytes 1622024 | tf_op jit(solution)/shard_map/ppermute | solution.py:311
  36.1 13.8 %collective-permute-start.4 = (f32[132,8,128]{2,1,0:T(8,128)S(1)}, f32[132,8,128]{2,1,0:T(8,128)S(1)}, u32[]{:S(2)}, u32[]{:S(2)}) collective-permute-start(f32[132,8,128]{2,1,0:T(8,128)S(1)} %get-tuple-element.15), channel_id=1, source_target_pairs={{0,16},{8,24},{16,0},{24,8},{1,17},{9,25},{17,1},{25,9},{2,18},{10... | collective-permute-start | bytes 1622024 | tf_op jit(solution)/shard_map/ppermute | solution.py:311
  37.3 15.3 %collective-permute-start.6 = (f32[16,66]{1,0:T(8,128)S(1)}, f32[16,66]{1,0:T(8,128)S(1)}, u32[]{:S(2)}, u32[]{:S(2)}) collective-permute-start(f32[16,66]{1,0:T(8,128)S(1)} %get-tuple-element.21), channel_id=1, source_target_pairs={{0,8},{8,16},{16,24},{24,0},{1,9},{9,17},{17,25},{25,1},{2,10},{10... | collective-permute-start | bytes 12680 | tf_op jit(solution)/shard_map/ppermute | solution.py:337
  37.9 14.7 %collective-permute-start.7 = (f32[16,66]{1,0:T(8,128)S(1)}, f32[16,66]{1,0:T(8,128)S(1)}, u32[]{:S(2)}, u32[]{:S(2)}) collective-permute-start(f32[16,66]{1,0:T(8,128)S(1)} %get-tuple-element.22), channel_id=1, source_target_pairs={{0,24},{8,0},{16,8},{24,16},{1,25},{9,1},{17,9},{25,17},{2,26},{10... | collective-permute-start | bytes 12680 | tf_op jit(solution)/shard_map/ppermute | solution.py:338
  48.7 13.9 %collective-permute-start.3 = (f32[132,8,128]{2,1,0:T(8,128)S(1)}, f32[132,8,128]{2,1,0:T(8,128)S(1)}, u32[]{:S(2)}, u32[]{:S(2)}) collective-permute-start(f32[132,8,128]{2,1,0:T(8,128)S(1)} %add.46.a0_ref), channel_id=1, source_target_pairs={{0,16},{8,24},{16,0},{24,8},{1,17},{9,25},{17,1},{25,9},{2,18},{10... | collective-permute-start | bytes 1622024 | tf_op jit(solution)/shard_map/ppermute | solution.py:311
  50.0 14.2 %collective-permute-start.5 = (f32[132,8,128]{2,1,0:T(8,128)S(1)}, f32[132,8,128]{2,1,0:T(8,128)S(1)}, u32[]{:S(2)}, u32[]{:S(2)}) collective-permute-start(f32[132,8,128]{2,1,0:T(8,128)S(1)} %add.47.b0_ref), channel_id=1, source_target_pairs={{0,8},{8,0},{16,24},{24,16},{1,9},{9,1},{17,25},{25,17},{2,10},{10... | collective-permute-start | bytes 1622024 | tf_op jit(solution)/shard_map/ppermute | solution.py:311
  87.3 13.2 %collective-permute-start.8 = (f32[128,8,128]{2,1,0:T(8,128)S(1)}, f32[128,8,128]{2,1,0:T(8,128)S(1)}, u32[]{:S(2)}, u32[]{:S(2)}) collective-permute-start(f32[128,8,128]{2,1,0:T(8,128)S(1)} %get-tuple-element.18), channel_id=1, source_target_pairs={{0,8},{8,0},{16,24},{24,16},{1,9},{9,1},{17,25},{25,17},{2,10},{10... | collective-permute-start | bytes 1572872 | tf_op jit(solution)/shard_map/ppermute | solution.py:311
  88.8 13.4 %collective-permute-start.10 = (f32[128,8,128]{2,1,0:T(8,128)S(1)}, f32[128,8,128]{2,1,0:T(8,128)S(1)}, u32[]{:S(2)}, u32[]{:S(2)}) collective-permute-start(f32[128,8,128]{2,1,0:T(8,128)S(1)} %get-tuple-element.19), channel_id=1, source_target_pairs={{0,16},{8,24},{16,0},{24,8},{1,17},{9,25},{17,1},{25,9},{2,18},{10... | collective-permute-start | bytes 1572872 | tf_op jit(solution)/shard_map/ppermute | solution.py:311
  100.5 14.4 %collective-permute-start.9 = (f32[128,8,128]{2,1,0:T(8,128)S(1)}, f32[128,8,128]{2,1,0:T(8,128)S(1)}, u32[]{:S(2)}, u32[]{:S(2)}) collective-permute-start(f32[128,8,128]{2,1,0:T(8,128)S(1)} %add.48.a0_ref), channel_id=1, source_target_pairs={{0,16},{8,24},{16,0},{24,8},{1,17},{9,25},{17,1},{25,9},{2,18},{10... | collective-permute-start | bytes 1572872 | tf_op jit(solution)/shard_map/ppermute | solution.py:311
  102.2 12.7 %collective-permute-start.11 = (f32[128,8,128]{2,1,0:T(8,128)S(1)}, f32[128,8,128]{2,1,0:T(8,128)S(1)}, u32[]{:S(2)}, u32[]{:S(2)}) collective-permute-start(f32[128,8,128]{2,1,0:T(8,128)S(1)} %add.49.b0_ref), channel_id=1, source_target_pairs={{0,8},{8,0},{16,24},{24,16},{1,9},{9,1},{17,25},{25,17},{2,10},{10... | collective-permute-start | bytes 1572872 | tf_op jit(solution)/shard_map/ppermute | solution.py:311
  104.8 9.9 %collective-permute-start.12 = (f32[16,64]{1,0:T(8,128)S(1)}, f32[16,64]{1,0:T(8,128)S(1)}, u32[]{:S(2)}, u32[]{:S(2)}) collective-permute-start(f32[16,64]{1,0:T(8,128)S(1)} %get-tuple-element.23), channel_id=1, source_target_pairs={{0,8},{8,16},{16,24},{24,0},{1,9},{9,17},{17,25},{25,1},{2,10},{10... | collective-permute-start | bytes 12296 | tf_op jit(solution)/shard_map/ppermute | solution.py:337
  106.3 8.4 %collective-permute-start.13 = (f32[16,64]{1,0:T(8,128)S(1)}, f32[16,64]{1,0:T(8,128)S(1)}, u32[]{:S(2)}, u32[]{:S(2)}) collective-permute-start(f32[16,64]{1,0:T(8,128)S(1)} %get-tuple-element.24), channel_id=1, source_target_pairs={{0,24},{8,0},{16,8},{24,16},{1,25},{9,1},{17,9},{25,17},{2,26},{10... | collective-permute-start | bytes 12296 | tf_op jit(solution)/shard_map/ppermute | solution.py:338
